TPU v7x, 512 devices: a whole 4x8x8 slice. The times are simulated.
512 devices in a mesh: tensor: 8 (over x, z_hi), seq: 64 (over z_lo, y, core).
Axes of the slice: x: 4, y: 8, z: 8 (z_hi: 2, z_lo: 4; z = z_hi * 4 + z_lo), core: 2. Of those that a mesh axis runs over, the one named last changes fastest.
Arguments:
- residual: bfloat16 [9728, 8192], P('seq', 'tensor'), may hold values from -6 to 6
- mean_vec: float32 [8192], replicated, may hold values from -6 to 6
- proj_u: float32 [8192], replicated, may hold values from -0.0625 to 0.0625
- proj_v: float32 [8192], replicated, may hold values from -6 to 6
- key_weight: bfloat16 [8192, 1024], P(None, 'tensor'), may hold values from -0.0625 to 0.0625
- value_weight: bfloat16 [8192, 1024], P(None, 'tensor'), may hold values from -0.0625 to 0.0625
- queries: bfloat16 [9728, 8192], P('seq', 'tensor'), may hold values from -110 to 110
- doc_ids: int32 [9728], P('seq'), may hold values from 0 to 3, never falling along the last dimension, each value on 1 to 4864 neighbouring positions
Outputs:
- attended: bfloat16 [9728, 8192], P('seq', 'tensor')
Inputs may be any that keep to these rules, and one draw needn't show every extreme that they name: `doc_ids`: document numbers never fall along the sequence; every document has at least one token and the longest has exactly 4864.
All inputs are finite; a program needn't handle non-finite values.
Results may differ from a plain program's by a relative error of at most 0.014.
The roundings to bfloat16 on the way count: a program that leaves them out, or rounds other values in their place, can miss the bound.
Values may be sent and summed in bfloat16 or wider, within the bound.
A program may use at most 128 MiB of HBM per device.

v0:
```python
import jax
import jax.numpy as jnp
from jax import lax
from jax.sharding import PartitionSpec as P

QUERY_HEADS = 64
KEY_VALUE_HEADS = 8
HEAD_SIZE = 128


def shifted(block, axis, distance):
    devices = range(lax.axis_size(axis))
    route = [(i - distance, i) for i in devices if i - distance in devices]
    return lax.ppermute(block, axis, route)


def on_device(residual, mean_vec, proj_u, proj_v, key_weight, value_weight, queries, doc_ids):
    tok_rows = residual.shape[0]
    part_width = residual.shape[1]
    offset = lax.axis_index("tensor") * part_width
    mean_part = lax.dynamic_slice_in_dim(mean_vec, offset, part_width)
    read_part = lax.dynamic_slice_in_dim(proj_u, offset, part_width)
    drop_part = lax.dynamic_slice_in_dim(proj_v, offset, part_width)
    local_rows = residual.astype(jnp.float32)
    partial_coef = jnp.dot(
        local_rows - mean_part[None, :], read_part, precision=lax.Precision.HIGHEST
    )
    coef = lax.psum(partial_coef, "tensor")
    erased_part = (local_rows - coef[:, None] * drop_part[None, :]).astype(jnp.bfloat16)
    erased = lax.all_gather(erased_part, "tensor", axis=1, tiled=True)
    keys = jnp.dot(erased, key_weight, preferred_element_type=jnp.float32).astype(jnp.bfloat16)
    values = jnp.dot(erased, value_weight, preferred_element_type=jnp.float32).astype(jnp.bfloat16)
    key_value = jnp.stack([keys, values])
    doc_table = lax.all_gather(doc_ids, "seq", axis=0, tiled=True)
    kv_local = key_weight.shape[1] // HEAD_SIZE
    head_group = QUERY_HEADS // KEY_VALUE_HEADS
    scale = 1.0 / HEAD_SIZE**0.5
    q_start = lax.axis_index("seq") * tok_rows
    q_pos = q_start + jnp.arange(tok_rows, dtype=jnp.int32)
    query_grid = queries.reshape(tok_rows, kv_local, head_group, HEAD_SIZE)

    def attend(carry, block, key_start):
        top_old, total_old, acc_old = carry
        count = block.shape[1]
        key_grid = block[0].reshape(count, kv_local, HEAD_SIZE)
        value_grid = block[1].reshape(count, kv_local, HEAD_SIZE)
        k_pos = key_start + jnp.arange(count, dtype=jnp.int32)
        k_doc = lax.dynamic_slice_in_dim(doc_table, key_start, count)
        allowed = (k_pos[None, :] <= q_pos[:, None]) & (k_doc[None, :] == doc_ids[:, None])
        score = (
            jnp.einsum("qkgd,tkd->kgqt", query_grid, key_grid, preferred_element_type=jnp.float32)
            * scale
        )
        score = jnp.where(allowed[None, None], score, -jnp.inf)
        top_new = jnp.maximum(top_old, jnp.max(score, axis=3))
        factor = jnp.exp(top_old - top_new)
        expo = jnp.exp(score - top_new[..., None])
        total_new = total_old * factor + jnp.sum(expo, axis=3)
        mixed = jnp.einsum(
            "kgqt,tkd->kgqd",
            expo.astype(jnp.bfloat16),
            value_grid,
            preferred_element_type=jnp.float32,
        )
        return (top_new, total_new, acc_old * factor[..., None] + mixed)

    def maybe_attend(carry, block, key_start, valid):
        count = block.shape[1]
        safe_start = jnp.clip(key_start, 0, doc_table.shape[0] - count)
        last_doc = lax.dynamic_slice_in_dim(doc_table, safe_start + count - 1, 1)[0]
        useful = valid & (key_start <= q_start + tok_rows - 1) & (last_doc >= doc_ids[0])
        return lax.cond(
            useful, lambda state: attend(state, block, safe_start), lambda state: state, carry
        )

    start_state = (
        jnp.full((kv_local, head_group, tok_rows), -1e30, jnp.float32),
        jnp.zeros((kv_local, head_group, tok_rows), jnp.float32),
        jnp.zeros((kv_local, head_group, tok_rows, HEAD_SIZE), jnp.float32),
    )
    seq_count = lax.axis_size("seq")
    own_index = lax.axis_index("seq")

    def open_step(step, state):
        carry, block = state
        source = own_index - step
        carry = maybe_attend(carry, block, source * tok_rows, source >= 0)
        return (carry, shifted(block, "seq", 1))

    carry, block = lax.fori_loop(0, seq_count - 1, open_step, (start_state, key_value))
    source = own_index - (seq_count - 1)
    carry = maybe_attend(carry, block, source * tok_rows, source >= 0)
    top_all, total_all, acc_all = carry
    result = acc_all / total_all[..., None]
    result = jnp.transpose(result, (2, 0, 1, 3)).reshape(
        tok_rows, kv_local * head_group * HEAD_SIZE
    )
    return result.astype(jnp.bfloat16)


def solution(mesh):
    return jax.shard_map(
        on_device,
        mesh=mesh,
        in_specs=(
            P("seq", "tensor"),
            P(),
            P(),
            P(),
            P(None, "tensor"),
            P(None, "tensor"),
            P("seq", "tensor"),
            P("seq"),
        ),
        out_specs=P("seq", "tensor"),
        check_vma=False,
    )
```

profile of v0, /device:TPU:192, one launch (start us, length us, event | category | flops | bytes accessed | tf_op | source)
XLA Modules:
  0.0 858.6 jit_solution(6538602270438531736)
XLA Ops:
  9.6 32.4 %psum.7 = f32[152]{0:T(256)S(1)} all-reduce(f32[152]{0:T(256)S(1)} %bitcast.117), channel_id=1, replica_groups=mesh['tensor'=8,'seq'=64] {'tensor'}, use_global_device_ids=true, to_apply=%region_0.0 | all-reduce | flops 152 | bytes 1216 | tf_op jit(solution)/shard_map/psum | solution.py:28
  47.6 227.3 %all-reduce = s32[9728]{0:T(1024)S(1)} all-reduce(s32[9728]{0:T(1024)S(1)} %dynamic-update-slice), channel_id=1, replica_groups=mesh['tensor'=8,'seq'=64] {'seq'}, use_global_device_ids=true, to_apply=%add | all-reduce | flops 9728 | bytes 77824
  280.8 569.9 %while.25 = (s32[]{:T(128)}, f32[1,8,152]{2,1,0:T(8,128)S(1)}, f32[1,8,152]{2,1,0:T(8,128)S(1)}, f32[1,8,152,128]{3,2,1,0:T(8,128)S(1)}, bf16[2,152,128]{2,1,0:T...) while((s32[]{:T(128)}, f32[1,8,152]{2,1,0:T(8,128)S(1)}, ...), condition=%wide.region_6.7_spmd.clone, body=%wide.region_1.6_spmd.clone.sunk | while | flops 96312384 | bytes 4449875 | solution.py:90
  291.1 4.2 collective-permute-start
  301.5 5.9 collective-permute-start
  313.6 4.2 collective-permute-start
  324.0 5.9 collective-permute-start
  336.0 4.2 collective-permute-start
  346.4 5.9 collective-permute-start
  358.5 5.4 collective-permute-start
  397.3 4.2 collective-permute-start
  416.7 4.2 collective-permute-start
  448.8 3.6 collective-permute-done
  457.5 3.6 collective-permute-done
  466.1 3.6 collective-permute-done
  474.8 3.6 collective-permute-done
  483.4 3.6 collective-permute-done
  492.1 3.6 collective-permute-done
  587.3 3.6 collective-permute-done
  596.0 3.6 collective-permute-done
  604.7 3.6 collective-permute-done
  751.8 3.6 collective-permute-done
  760.5 3.6 collective-permute-done
  769.2 3.6 collective-permute-done
  (582 shorter events, 455.2 us)
Async XLA Ops:
  6.5 270.3 %all-gather.2.cloned.1.call-start = ((), (), s32[]{:S(2)}) async-start(), calls=%async_computation | async-start | bytes 2801664 | tf_op jit(solution)/shard_map/all_gather | solution.py:30
  281.5 9.0 %collective-permute-start = (bf16[2,152,128]{2,1,0:T(8,128)(2,1)}, bf16[2,152,128]{2,1,0:T(8,128)(2,1)S(1)}, u32[]{:S(2)}, u32[]{:S(2)}) collective-permute-start(bf16[2,152,128]{2,1,0:T(8,128)(2,1)} %copy.45), channel_id=1, source_target_pairs={{0,1},{1,2},{2,3},{3,4},{4,5},{5,6},{6,7},{7,8},{8,9},{9,10},{10,1... | collective-permute-start | bytes 233480 | tf_op jit(solution)/shard_map/while/body/eval_jaxpr/ppermute | solution.py:14
  291.1 9.7 %collective-permute-start = (bf16[2,152,128]{2,1,0:T(8,128)(2,1)}, bf16[2,152,128]{2,1,0:T(8,128)(2,1)S(1)}, u32[]{:S(2)}, u32[]{:S(2)}) collective-permute-start(bf16[2,152,128]{2,1,0:T(8,128)(2,1)} %copy.45), channel_id=1, source_target_pairs={{0,1},{1,2},{2,3},{3,4},{4,5},{5,6},{6,7},{7,8},{8,9},{9,10},{10,1... | collective-permute-start | bytes 233480 | tf_op jit(solution)/shard_map/while/body/eval_jaxpr/ppermute | solution.py:14
  301.5 11.4 %collective-permute-start = (bf16[2,152,128]{2,1,0:T(8,128)(2,1)}, bf16[2,152,128]{2,1,0:T(8,128)(2,1)S(1)}, u32[]{:S(2)}, u32[]{:S(2)}) collective-permute-start(bf16[2,152,128]{2,1,0:T(8,128)(2,1)} %copy.45), channel_id=1, source_target_pairs={{0,1},{1,2},{2,3},{3,4},{4,5},{5,6},{6,7},{7,8},{8,9},{9,10},{10,1... | collective-permute-start | bytes 233480 | tf_op jit(solution)/shard_map/while/body/eval_jaxpr/ppermute | solution.py:14
  313.6 9.7 %collective-permute-start = (bf16[2,152,128]{2,1,0:T(8,128)(2,1)}, bf16[2,152,128]{2,1,0:T(8,128)(2,1)S(1)}, u32[]{:S(2)}, u32[]{:S(2)}) collective-permute-start(bf16[2,152,128]{2,1,0:T(8,128)(2,1)} %copy.45), channel_id=1, source_target_pairs={{0,1},{1,2},{2,3},{3,4},{4,5},{5,6},{6,7},{7,8},{8,9},{9,10},{10,1... | collective-permute-start | bytes 233480 | tf_op jit(solution)/shard_map/while/body/eval_jaxpr/ppermute | solution.py:14
  324.0 11.4 %collective-permute-start = (bf16[2,152,128]{2,1,0:T(8,128)(2,1)}, bf16[2,152,128]{2,1,0:T(8,128)(2,1)S(1)}, u32[]{:S(2)}, u32[]{:S(2)}) collective-permute-start(bf16[2,152,128]{2,1,0:T(8,128)(2,1)} %copy.45), channel_id=1, source_target_pairs={{0,1},{1,2},{2,3},{3,4},{4,5},{5,6},{6,7},{7,8},{8,9},{9,10},{10,1... | collective-permute-start | bytes 233480 | tf_op jit(solution)/shard_map/while/body/eval_jaxpr/ppermute | solution.py:14
  336.0 9.7 %collective-permute-start = (bf16[2,152,128]{2,1,0:T(8,128)(2,1)}, bf16[2,152,128]{2,1,0:T(8,128)(2,1)S(1)}, u32[]{:S(2)}, u32[]{:S(2)}) collective-permute-start(bf16[2,152,128]{2,1,0:T(8,128)(2,1)} %copy.45), channel_id=1, source_target_pairs={{0,1},{1,2},{2,3},{3,4},{4,5},{5,6},{6,7},{7,8},{8,9},{9,10},{10,1... | collective-permute-start | bytes 233480 | tf_op jit(solution)/shard_map/while/body/eval_jaxpr/ppermute | solution.py:14
  346.4 11.4 %collective-permute-start = (bf16[2,152,128]{2,1,0:T(8,128)(2,1)}, bf16[2,152,128]{2,1,0:T(8,128)(2,1)S(1)}, u32[]{:S(2)}, u32[]{:S(2)}) collective-permute-start(bf16[2,152,128]{2,1,0:T(8,128)(2,1)} %copy.45), channel_id=1, source_target_pairs={{0,1},{1,2},{2,3},{3,4},{4,5},{5,6},{6,7},{7,8},{8,9},{9,10},{10,1... | collective-permute-start | bytes 233480 | tf_op jit(solution)/shard_map/while/body/eval_jaxpr/ppermute | solution.py:14
  358.5 10.9 %collective-permute-start = (bf16[2,152,128]{2,1,0:T(8,128)(2,1)}, bf16[2,152,128]{2,1,0:T(8,128)(2,1)S(1)}, u32[]{:S(2)}, u32[]{:S(2)}) collective-permute-start(bf16[2,152,128]{2,1,0:T(8,128)(2,1)} %copy.45), channel_id=1, source_target_pairs={{0,1},{1,2},{2,3},{3,4},{4,5},{5,6},{6,7},{7,8},{8,9},{9,10},{10,1... | collective-permute-start | bytes 233480 | tf_op jit(solution)/shard_map/while/body/eval_jaxpr/ppermute | solution.py:14
  378.7 8.9 %collective-permute-start = (bf16[2,152,128]{2,1,0:T(8,128)(2,1)}, bf16[2,152,128]{2,1,0:T(8,128)(2,1)S(1)}, u32[]{:S(2)}, u32[]{:S(2)}) collective-permute-start(bf16[2,152,128]{2,1,0:T(8,128)(2,1)} %copy.45), channel_id=1, source_target_pairs={{0,1},{1,2},{2,3},{3,4},{4,5},{5,6},{6,7},{7,8},{8,9},{9,10},{10,1... | collective-permute-start | bytes 233480 | tf_op jit(solution)/shard_map/while/body/eval_jaxpr/ppermute | solution.py:14
  388.3 8.4 collective-permute-start
  397.3 9.7 %collective-permute-start = (bf16[2,152,128]{2,1,0:T(8,128)(2,1)}, bf16[2,152,128]{2,1,0:T(8,128)(2,1)S(1)}, u32[]{:S(2)}, u32[]{:S(2)}) collective-permute-start(bf16[2,152,128]{2,1,0:T(8,128)(2,1)} %copy.45), channel_id=1, source_target_pairs={{0,1},{1,2},{2,3},{3,4},{4,5},{5,6},{6,7},{7,8},{8,9},{9,10},{10,1... | collective-permute-start | bytes 233480 | tf_op jit(solution)/shard_map/while/body/eval_jaxpr/ppermute | solution.py:14
  407.7 8.4 collective-permute-start
  416.7 9.7 %collective-permute-start = (bf16[2,152,128]{2,1,0:T(8,128)(2,1)}, bf16[2,152,128]{2,1,0:T(8,128)(2,1)S(1)}, u32[]{:S(2)}, u32[]{:S(2)}) collective-permute-start(bf16[2,152,128]{2,1,0:T(8,128)(2,1)} %copy.45), channel_id=1, source_target_pairs={{0,1},{1,2},{2,3},{3,4},{4,5},{5,6},{6,7},{7,8},{8,9},{9,10},{10,1... | collective-permute-start | bytes 233480 | tf_op jit(solution)/shard_map/while/body/eval_jaxpr/ppermute | solution.py:14
  427.1 8.0 collective-permute-start
  435.7 8.0 collective-permute-start
  444.4 8.0 collective-permute-start
  582.9 8.0 collective-permute-start
  591.6 8.0 collective-permute-start
  600.3 8.0 collective-permute-start
  608.9 8.0 collective-permute-start
  747.4 8.0 collective-permute-start
  756.1 8.0 collective-permute-start
  764.8 8.0 collective-permute-start
  (45 other events, 671.6 us)
Sparse Core Ops, SparseCore 0:
  44.7 82.0 all-gather.1
where the time goes:
time: 866 us; the launch traced here: 859 us
  blocking collectives  260 us (30%)
  waiting for transfers between devices  177 us (20%)
  starting transfers between devices  153 us (18%)
  local copies, waits for them, and re-layouts  121 us (14%)
  loops' own time  84.3 us (10%)
  matrix products  40.8 us (5%)
  between operations  15.5 us (2%)
    unnamed x1, blocking collectives  227 us
    ppermute x63, waiting for transfers between devices, shifted(): return lax.ppermute(block, axis, route)  177 us
    ppermute x63, starting transfers between devices, shifted(): return lax.ppermute(block, axis, route)  153 us
    another operation x1, loops' own time, on_device(): lax.fori_loop(0, seq_count - 1, open_step, (start_state, key_value))  82.5 us
    while x63, local copies, waits for them, and re-layouts  40 us
    slice x64, local copies, waits for them, and re-layouts, maybe_attend(): doc_ids[0]  37.9 us
    dynamic_slice x64, local copies, waits for them, and re-layouts, maybe_attend(): last_doc = lax.dynamic_slice_in_dim(doc_table, safe_start + count - 1, 1)[0]  36.9 us
    psum x1, blocking collectives, on_device(): coef = lax.psum(partial_coef, 'tensor')  32.4 us
  transfers between devices with their start and end apart: 64, of which 50 were waited for; matrix products, arithmetic and copies ran while one was open for 14% of the time, Pallas kernels for 0%

commit v1 on v0

v1 whole, which is shorter than its diff:
```python
import functools
import jax
import jax.numpy as jnp
from jax import lax
from jax.experimental import pallas as pl
from jax.experimental.pallas import tpu as pltpu
from jax.sharding import PartitionSpec as P

HEADS = 8
HEAD = 128
TOK = 152
ROWS = 160
CUT = ((0, 80), (80, 80))
WIDTH = 1024
YN = 8
SCALE = 1.0 / HEAD**0.5
FAR = -1e30
MESH = pl.DeviceIdType.MESH
OWN, MATE = 4 * YN, 4 * YN + 1
SLOTS = 4 * YN + 2
SEMS = 96


def kernel(
    res, mean, read, drop, wk_hbm, wv_hbm, qry, doc, out,
    rbuf, wbuf, kvbuf, qbuf, kx, vx, acc, top, ssem, rsem, wsem,
):
    t = lax.axis_index("tensor")
    s = lax.axis_index("seq")
    x, zh = t // 2, t % 2
    zl, y, core = s // 16, (s // 2) % YN, s % 2

    def dev(x_, zh_, zl_, y_, core_):
        return (x_ * 2 + zh_, zl_ * 16 + y_ * 2 + core_)

    right = dev((x + 1) % 4, zh, zl, y, core)
    left = dev((x + 3) % 4, zh, zl, y, core)
    across = dev(x, 1 - zh, zl, y, core)
    above = dev(x, zh, (zl + 1) % 4, y, core)
    below = dev(x, zh, (zl + 3) % 4, y, core)
    mate = dev(x, zh, zl, y, 1 - core)
    has_above, has_below = zl < 3, zl > 0

    def ring(d):
        return dev(x, zh, zl, (y + d) % YN, core)

    bar = pltpu.get_barrier_semaphore()

    def hello(device):
        pl.semaphore_signal(bar, inc=1, device_id=device, device_id_type=MESH)

    for device in [right, left, across, mate] + [ring(d) for d in range(1, YN)]:
        hello(device)

    @pl.when(has_above)
    def _():
        hello(above)

    @pl.when(has_below)
    def _():
        hello(below)

    wcopies = [
        pltpu.make_async_copy(wk_hbm, wbuf.at[:, pl.ds(0, HEAD)], wsem.at[0]),
        pltpu.make_async_copy(wv_hbm, wbuf.at[:, pl.ds(HEAD, HEAD)], wsem.at[1]),
    ]
    for cp in wcopies:
        cp.start()

    def padded(value):
        wide = value.astype(jnp.float32)
        tail = jnp.zeros((ROWS - TOK, wide.shape[1]), jnp.float32)
        return jnp.concatenate([wide, tail], axis=0).astype(jnp.bfloat16)

    rbuf[0] = padded(res[...])
    lane = lax.broadcasted_iota(jnp.int32, (1, HEAD), 1)
    docs = doc[...]
    low = jnp.zeros((1, HEAD), jnp.float32)
    high = jnp.zeros((1, HEAD), jnp.float32)
    for d in range(4):
        under = jnp.sum((docs < d).astype(jnp.float32), axis=1, keepdims=True)
        upto = jnp.sum((docs <= d).astype(jnp.float32), axis=1, keepdims=True)
        low = jnp.where(lane == d, under, low)
        high = jnp.where(lane == d, upto, high)
    row_at = lax.broadcasted_iota(jnp.int32, (ROWS, HEAD), 0).astype(jnp.float32)
    inside = (row_at >= low) & (row_at < high)
    q_mark = jnp.where(inside, FAR, 0.0).astype(jnp.bfloat16)
    for h in range(HEADS):
        qbuf[h, :, 0:HEAD] = padded(qry[:, h * HEAD:(h + 1) * HEAD])
        qbuf[h, :, HEAD:2 * HEAD] = q_mark
    empty = jnp.zeros((ROWS, 2 * HEAD), jnp.bfloat16)

    @pl.when(core == 0)
    def _():
        kvbuf[MATE] = empty

    @pl.when(zl == 0)
    def _():
        kvbuf[0] = empty
        for d in range(YN):
            kvbuf[4 * d + 1] = empty

    vx[:, HEAD:2 * HEAD] = jnp.ones((4 * ROWS, HEAD), jnp.bfloat16)

    peers = 4 + YN - 1 + jnp.where(has_above, 1, 0) + jnp.where(has_below, 1, 0)
    pl.semaphore_wait(bar, peers)

    used = [0]
    sent = []

    def copy(buf, src, dst, cut, device):
        i = used[0]
        used[0] += 1
        first, rows = cut
        return pltpu.make_async_remote_copy(
            src_ref=buf.at[src, pl.ds(first, rows)],
            dst_ref=buf.at[dst, pl.ds(first, rows)],
            send_sem=ssem.at[i],
            recv_sem=rsem.at[i],
            device_id=device,
            device_id_type=MESH,
        )

    def go(cp, when=None):
        sent.append((cp, when))
        if when is None:
            cp.start()
        else:
            pl.when(when)(cp.start)

    def got(cp, when=None):
        if when is None:
            cp.wait_recv()
        else:
            pl.when(when)(cp.wait_recv)

    over = [copy(rbuf, 0, 4, cut, across) for cut in CUT]
    to_right = [[copy(rbuf, 4 * h, 4 * h + 1, cut, right) for cut in CUT] for h in range(2)]
    to_left = [[copy(rbuf, 4 * h, 4 * h + 2, cut, left) for cut in CUT] for h in range(2)]
    onward = [
        [copy(rbuf, 4 * h + 1, 4 * h + 3, CUT[0], right), copy(rbuf, 4 * h + 2, 4 * h + 3, CUT[1], left)]
        for h in range(2)
    ]
    for c in range(2):
        go(over[c])
    for c in range(2):
        go(to_right[0][c])
        go(to_left[0][c])
    got(to_right[0][0])
    go(onward[0][0])
    got(to_left[0][0])
    got(to_left[0][1])
    go(onward[0][1])
    got(to_right[0][1])
    for c in range(2):
        got(over[c])
        go(to_right[1][c])
        go(to_left[1][c])
    got(onward[0][0])
    got(onward[0][1])
    got(to_right[1][0])
    go(onward[1][0])
    got(to_left[1][0])

    whose = [(x * 2 + zh), ((x + 3) % 4) * 2 + zh, ((x + 1) % 4) * 2 + zh, ((x + 2) % 4) * 2 + zh]
    whose = whose + [w + 1 - 2 * zh for w in whose]

    def project(c):
        first, rows = CUT[c]
        part = jnp.zeros((rows, HEAD), jnp.float32)
        for slot in range(8):
            block = rbuf[slot, first:first + rows, :].astype(jnp.float32)
            term = (block - mean[whose[slot]]) * read[whose[slot]]
            for j in range(WIDTH // HEAD):
                part = part + term[:, j * HEAD:(j + 1) * HEAD]
        coef = jnp.sum(part, axis=1, keepdims=True)
        total = jnp.zeros((rows, 2 * HEAD), jnp.float32)
        for slot in range(8):
            block = rbuf[slot, first:first + rows, :].astype(jnp.float32)
            erased = (block - coef * drop[whose[slot]]).astype(jnp.bfloat16)
            weight = wbuf[pl.ds(pl.multiple_of(whose[slot] * WIDTH, WIDTH), WIDTH), :]
            total = total + jnp.dot(erased, weight, preferred_element_type=jnp.float32)
        if first + rows > TOK:
            at = lax.broadcasted_iota(jnp.int32, (rows, 2 * HEAD), 0) + first
            blank = jnp.zeros((1, HEAD), jnp.float32)
            low2 = jnp.concatenate([low, blank], axis=1)
            high2 = jnp.concatenate([high, blank], axis=1)
            total = jnp.where(at >= TOK, jnp.where(at == TOK, low2, jnp.where(at == TOK + 1, high2, 0.0)), total)
        kvbuf[OWN, first:first + rows, :] = total.astype(jnp.bfloat16)

    up = [copy(kvbuf, OWN, 0, cut, above) for cut in CUT]
    up2 = [copy(kvbuf, 0, 1, cut, above) for cut in CUT]
    near = [
        [copy(kvbuf, jnp.where(y + d < YN, OWN, 0), 4 * d, cut, ring(d)) for cut in CUT]
        for d in range(1, YN)
    ]
    far = [[copy(kvbuf, 4 * d, 4 * d + 1, cut, above) for cut in CUT] for d in range(1, YN)]
    side = [copy(kvbuf, OWN, MATE, cut, mate) for cut in CUT]
    used_side = [used[0]]

    def pair(d, c):
        i = used[0]
        used[0] += 1
        first, rows = CUT[c]
        return pltpu.make_async_remote_copy(
            src_ref=kvbuf.at[pl.ds(4 * d, 2), pl.ds(first, rows)],
            dst_ref=kvbuf.at[pl.ds(4 * d + 2, 2), pl.ds(first, rows)],
            send_sem=ssem.at[i],
            recv_sem=rsem.at[i],
            device_id=mate,
            device_id_type=MESH,
        )

    pairs = [[pair(d, c) for c in range(2)] for d in range(YN)]
    order = sorted(range(1, YN), key=lambda d: min(d, YN - d))

    def share(c):
        go(up[c], has_above)
        for d in order:
            go(near[d - 1][c], y + d < YN)
        go(side[c], core == 0)

    def wrapped(c):
        got(up[c], has_below)
        go(up2[c], has_above)
        for d in order:
            go(near[d - 1][c], y + d >= YN)

    def relay(c, d):
        got(near[d - 1][c])
        go(far[d - 1][c], has_above)

    for cp in wcopies:
        cp.wait()
    got(onward[1][0])
    project(0)
    share(0)
    got(to_left[1][1])
    go(onward[1][1])
    got(to_right[1][1])
    wrapped(0)
    got(onward[1][1])
    project(1)
    share(1)
    for d in order:
        relay(0, d)
    wrapped(1)
    for c in range(2):
        got(up2[c], has_below)
        go(pairs[0][c])

    def attend(slot0, blocks, start):
        keys = blocks * ROWS
        for i in range(blocks):
            rows = slice(i * ROWS, (i + 1) * ROWS)
            block = kvbuf[slot0 + i]
            kx[rows, 0:HEAD] = block[:, 0:HEAD]
            vx[rows, 0:HEAD] = block[:, HEAD:2 * HEAD]
            tail = kvbuf[slot0 + i, 144:160, 0:HEAD].astype(jnp.float32)
            seen = (row_at >= tail[8:9]) & (row_at < tail[9:10])
            kx[rows, HEAD:2 * HEAD] = jnp.where(seen, 0.0, 1.0).astype(jnp.bfloat16)

        def one(h, carry):
            score = lax.dot_general(
                qbuf[h], kx[0:keys], (((1,), (1,)), ((), ())), preferred_element_type=jnp.float32
            )
            if start:
                q_at = lax.broadcasted_iota(jnp.int32, (ROWS, keys), 0)
                k_at = lax.broadcasted_iota(jnp.int32, (ROWS, keys), 1)
                score = jnp.where((k_at <= q_at) | (k_at >= ROWS), score, FAR)
            best = jnp.max(score, axis=1, keepdims=True)
            if not start:
                old = top[h][:, 0:1]
                best = jnp.maximum(best, old)
            expo = jnp.exp((score - best) * SCALE).astype(jnp.bfloat16)
            mixed = jnp.dot(expo, vx[0:keys], preferred_element_type=jnp.float32)
            if not start:
                mixed = mixed + acc[h] * jnp.exp((old - best) * SCALE)
            acc[h] = mixed
            top[h] = jnp.broadcast_to(best, (ROWS, HEAD))
            return carry

        lax.fori_loop(0, HEADS, one, 0)

    for c in range(2):
        got(side[c], core == 1)
    attend(OWN, 2, True)
    for d in order:
        relay(1, d)
        for c in range(2):
            got(far[d - 1][c], has_below)
            go(pairs[d][c])
    for c in range(2):
        got(pairs[0][c])
    attend(0, 4, False)
    for d in order:
        for c in range(2):
            got(pairs[d][c])
        attend(4 * d, 4, False)

    for h in range(HEADS):
        both = acc[h]
        out[:, h * HEAD:(h + 1) * HEAD] = (both[0:TOK, 0:HEAD] / both[0:TOK, HEAD:2 * HEAD]).astype(jnp.bfloat16)

    for cp, when in sent:
        if when is None:
            cp.wait_send()
        else:
            pl.when(when)(cp.wait_send)


def on_device(residual, mean_vec, proj_u, proj_v, key_weight, value_weight, queries, doc_ids):
    whole = pl.BlockSpec(memory_space=pltpu.VMEM)
    hbm = pl.BlockSpec(memory_space=pl.ANY)
    flat = (8, 1, WIDTH)
    return pl.pallas_call(
        kernel,
        out_shape=jax.ShapeDtypeStruct((TOK, WIDTH), jnp.bfloat16),
        in_specs=[whole, whole, whole, whole, hbm, hbm, whole, whole],
        out_specs=whole,
        scratch_shapes=[
            pltpu.VMEM((8, ROWS, WIDTH), jnp.bfloat16),
            pltpu.VMEM((8 * WIDTH, 2 * HEAD), jnp.bfloat16),
            pltpu.VMEM((SLOTS, ROWS, 2 * HEAD), jnp.bfloat16),
            pltpu.VMEM((HEADS, ROWS, 2 * HEAD), jnp.bfloat16),
            pltpu.VMEM((4 * ROWS, 2 * HEAD), jnp.bfloat16),
            pltpu.VMEM((4 * ROWS, 2 * HEAD), jnp.bfloat16),
            pltpu.VMEM((HEADS, ROWS, 2 * HEAD), jnp.float32),
            pltpu.VMEM((HEADS, ROWS, HEAD), jnp.float32),
            pltpu.SemaphoreType.DMA((SEMS,)),
            pltpu.SemaphoreType.DMA((SEMS,)),
            pltpu.SemaphoreType.DMA((2,)),
        ],
        compiler_params=pltpu.CompilerParams(
            collective_id=0, has_side_effects=True, vmem_limit_bytes=48 << 20
        ),
    )(
        residual, mean_vec.reshape(flat), proj_u.reshape(flat), proj_v.reshape(flat),
        key_weight, value_weight, queries, doc_ids.reshape(1, TOK),
    )


def solution(mesh):
    return jax.shard_map(
        on_device,
        mesh=mesh,
        in_specs=(
            P("seq", "tensor"), P(), P(), P(), P(None, "tensor"), P(None, "tensor"),
            P("seq", "tensor"), P("seq"),
        ),
        out_specs=P("seq", "tensor"),
        check_vma=False,
    )
```

time: 866 us -> 118 us (0.14)
  blocking collectives: 260 us -> 0 us
  waiting for transfers between devices: 177 us -> 0 us
  starting transfers between devices: 153 us -> 0 us
  local copies, waits for them, and re-layouts: 121 us -> 8.79 us
  Pallas kernels: 0 us -> 108 us
  loops' own time: 84.3 us -> 0 us
  matrix products: 40.8 us -> 0 us
  between operations: 15.5 us -> 0.02 us
    unnamed x1 -> x0, blocking collectives: 227 us -> none
    ppermute x63 -> x0, waiting for transfers between devices: 177 us -> none  [shifted(): return lax.ppermute(block, axis, route)]
    ppermute x63 -> x0, starting transfers between devices: 153 us -> none  [shifted(): return lax.ppermute(block, axis, route)]
    pallas_call x0 -> x1, Pallas kernels: none -> 108 us  [on_device(): pl.pallas_call(kernel, out_shape=jax.ShapeDtypeStruct((TOK, WIDTH), jnp.b...]
    another operation x65 -> x0, loops' own time: 84.3 us -> none  [the longest x1 82.5 us: on_device(): lax.fori_loop(0, seq_count - 1, open_step, (start_state, key_value))]
    dot_general x31 -> x0, matrix products: 40.8 us -> none  [the longest x14 20 us: attend(): jnp.einsum('kgqt,tkd->kgqd', expo.astype(jnp.bfloat16), value_grid, prefe...]
    dynamic_slice x81 -> x0, local copies, waits for them, and re-layouts: 40.3 us -> none  [the longest x64 36.9 us: maybe_attend(): last_doc = lax.dynamic_slice_in_dim(doc_table, safe_start + count - 1, 1)[0]]
    while x63 -> x0, local copies, waits for them, and re-layouts: 40 us -> none
  transfers between devices with their start and end apart: 64 -> 0, of which waited for: 50 -> 0; matrix products, arithmetic and copies ran while one was open for 14% -> 0% of each run, Pallas kernels for 0% -> 0%
where the time goes in v1:
time: 118 us; the launch traced here: 117 us
  Pallas kernels  108 us (92%)
  local copies, waits for them, and re-layouts  8.79 us (7%)
    pallas_call x1, Pallas kernels, on_device(): pl.pallas_call(kernel, out_shape=jax.ShapeDtypeStruct((TOK, WIDTH), jnp.b...  108 us
    unnamed x17, local copies, waits for them, and re-layouts  8.79 us

profile of v1, /device:TPU:192, one launch (start us, length us, event | category | flops | bytes accessed | tf_op | source)
XLA Modules:
  0.0 117.2 jit_solution(11563575806822845498)
XLA Ops:
  0.0 0.0 copy-start
  0.0 1.6 %copy-done = bf16[8192,128]{1,0:T(8,128)(2,1)S(1)} copy-done((bf16[8192,128]{1,0:T(8,128)(2,1)S(1)}, bf16[8192,128]{1,0:T(8,128)(2,1)}, u32[]{:S(2)}) %copy-start) | copy-done | bytes 2097176
  1.6 0.0 copy-start.1
  1.6 1.6 %copy-done.1 = bf16[8192,128]{1,0:T(8,128)(2,1)S(1)} copy-done((bf16[8192,128]{1,0:T(8,128)(2,1)S(1)}, bf16[8192,128]{1,0:T(8,128)(2,1)}, u32[]{:S(2)}) %copy-start.1) | copy-done | bytes 2097176
  3.2 0.0 copy-start.2
  3.2 1.0 copy-done.2
  4.2 0.0 copy-start.3
  4.2 1.0 copy-done.3
  5.1 0.0 copy-start.4
  5.1 0.8 copy-done.4
  5.9 0.0 copy-start.5
  5.9 0.8 copy-done.5
  6.6 0.0 copy-start.6
  6.6 0.8 copy-done.6
  7.4 0.0 copy-start.7
  7.4 0.7 copy-done.7
  8.1 108.4 %shard_map.82 = bf16[152,1024]{1,0:T(8,128)(2,1)S(1)} custom-call(bf16[152,1024]{1,0:T(8,128)(2,1)S(1)} %copy-done.2, f32[8,1,1024]{2,1,0:T(1,128)S(1)} %bitcast.4, f32[8,1,1024]{2,1,0:T(1,128)S(1)} %bitcast.5, f32[8,1,1024]{2,1,0:T(1,128)S(1)} %bitcast.6, bf16[8192,128]{1,0:T(8,128)(2,1)S(1)} %copy-done, bf16[8192,128]{1,0:T(8,128)(2,1)S(1)} %copy-done.1, ...), custom_call_target="tpu_custom_call" | custom-call | tf_op jit(solution)/shard_map/pallas_call | solution.py:316
  116.5 0.7 copy.10
Async XLA Ops:
  0.0 1.6 %copy-start = (bf16[8192,128]{1,0:T(8,128)(2,1)S(1)}, bf16[8192,128]{1,0:T(8,128)(2,1)}, u32[]{:S(2)}) copy-start(bf16[8192,128]{1,0:T(8,128)(2,1)} %wk_hbm.1) | copy-start | bytes 6291460
  1.6 1.6 %copy-start.1 = (bf16[8192,128]{1,0:T(8,128)(2,1)S(1)}, bf16[8192,128]{1,0:T(8,128)(2,1)}, u32[]{:S(2)}) copy-start(bf16[8192,128]{1,0:T(8,128)(2,1)} %wv_hbm.1) | copy-start | bytes 6291460
  3.2 1.0 copy-start.2
  4.2 1.0 copy-start.3
  5.1 0.8 copy-start.4
  5.9 0.8 copy-start.5
  6.6 0.8 copy-start.6
  7.4 0.7 copy-start.7

commit v2 on v1

v2 whole, which is shorter than its diff:
```python
import functools
import jax
import jax.numpy as jnp
from jax import lax
from jax.experimental import pallas as pl
from jax.experimental.pallas import tpu as pltpu
from jax.sharding import PartitionSpec as P

HEADS = 8
HEAD = 128
TOK = 152
ROWS = 160
GAP = 72
CUT = ((0, 80), (80, 80))
PIECE = ((0, 48), (48, 32), (80, 48), (128, 32))
WIDTH = 1024
YN = 8
SCALE = 1.0 / HEAD**0.5
LOG2E = 1.4426950408889634
FAR = -1e30
MESH = pl.DeviceIdType.MESH
OWN, MATE = 4 * YN, 4 * YN + 1
SLOTS = 4 * YN + 2
SEMS = 96


def kernel(
    res_hbm, mean_hbm, read_hbm, drop_hbm, wk_hbm, wv_hbm, qry_hbm, doc_hbm, out,
    res, mean, read, drop, qry, doc,
    rbuf, wbuf, kvbuf, qbuf, kx, vx, acc, top, ssem, rsem, wsem,
):
    t = lax.axis_index("tensor")
    s = lax.axis_index("seq")
    x, zh = t // 2, t % 2
    zl, y, core = s // 16, (s // 2) % YN, s % 2

    def dev(x_, zh_, zl_, y_, core_):
        return (x_ * 2 + zh_, zl_ * 16 + y_ * 2 + core_)

    right = dev((x + 1) % 4, zh, zl, y, core)
    left = dev((x + 3) % 4, zh, zl, y, core)
    across = dev(x, 1 - zh, zl, y, core)
    above = dev(x, zh, (zl + 1) % 4, y, core)
    below = dev(x, zh, (zl + 3) % 4, y, core)
    mate = dev(x, zh, zl, y, 1 - core)
    has_above, has_below = zl < 3, zl > 0

    def ring(d):
        return dev(x, zh, zl, (y + d) % YN, core)

    bar = pltpu.get_barrier_semaphore()

    def hello(device):
        pl.semaphore_signal(bar, inc=1, device_id=device, device_id_type=MESH)

    for device in [right, left, across, mate] + [ring(d) for d in range(1, YN)]:
        hello(device)

    @pl.when(has_above)
    def _():
        hello(above)

    @pl.when(has_below)
    def _():
        hello(below)

    loads = [
        pltpu.make_async_copy(src, dst, wsem.at[i])
        for i, (src, dst) in enumerate([
            (res_hbm, res), (doc_hbm, doc), (qry_hbm, qry), (mean_hbm, mean), (read_hbm, read), (drop_hbm, drop),
            (wk_hbm, wbuf.at[:, pl.ds(0, HEAD)]), (wv_hbm, wbuf.at[:, pl.ds(HEAD, HEAD)]),
        ])
    ]
    for cp in loads:
        cp.start()

    def padded(value):
        wide = value.astype(jnp.float32)
        blank = jnp.zeros((ROWS - TOK, wide.shape[1]), jnp.float32)
        return jnp.concatenate([wide[:GAP], blank, wide[GAP:]], axis=0).astype(jnp.bfloat16)

    empty = jnp.zeros((ROWS, 2 * HEAD), jnp.bfloat16)

    @pl.when(core == 0)
    def _():
        kvbuf[MATE] = empty

    @pl.when(zl == 0)
    def _():
        kvbuf[0] = empty
        for d in range(YN):
            kvbuf[4 * d + 1] = empty

    loads[0].wait()
    rbuf[0] = padded(res[...])

    peers = 4 + YN - 1 + jnp.where(has_above, 1, 0) + jnp.where(has_below, 1, 0)
    pl.semaphore_wait(bar, peers)

    used = [0]
    sent = []

    def copy(buf, src, dst, cut, device):
        i = used[0]
        used[0] += 1
        first, rows = cut
        return pltpu.make_async_remote_copy(
            src_ref=buf.at[src, pl.ds(first, rows)],
            dst_ref=buf.at[dst, pl.ds(first, rows)],
            send_sem=ssem.at[i],
            recv_sem=rsem.at[i],
            device_id=device,
            device_id_type=MESH,
        )

    def go(cp, when=None):
        sent.append((cp, when))
        if when is None:
            cp.start()
        else:
            pl.when(when)(cp.start)

    def got(cp, when=None):
        if when is None:
            cp.wait_recv()
        else:
            pl.when(when)(cp.wait_recv)

    over = [copy(rbuf, 0, 4, cut, across) for cut in PIECE]
    to_right = [[copy(rbuf, 4 * h, 4 * h + 1, cut, right) for cut in (CUT, PIECE)[h]] for h in range(2)]
    to_left = [[copy(rbuf, 4 * h, 4 * h + 2, cut, left) for cut in (CUT, PIECE)[h]] for h in range(2)]
    rightward = ((True, False), (True, False, False, True))
    onward = [
        [
            copy(rbuf, 4 * h + 1, 4 * h + 3, cut, right) if way else copy(rbuf, 4 * h + 2, 4 * h + 3, cut, left)
            for way, cut in zip(rightward[h], (CUT, PIECE)[h])
        ]
        for h in range(2)
    ]

    def spread(h, p):
        go(to_right[h][p])
        go(to_left[h][p])

    def carry_on(h, p):
        got((to_right if rightward[h][p] else to_left)[h][p])
        go(onward[h][p])

    def rest(h, p):
        got((to_left if rightward[h][p] else to_right)[h][p])
        got(onward[h][p])

    go(over[0])
    spread(0, 0)
    go(over[1])
    spread(0, 1)
    for cp in loads[1:3]:
        cp.wait()
    lane = lax.broadcasted_iota(jnp.int32, (1, HEAD), 1)
    docs = doc[...]
    low = jnp.zeros((1, HEAD), jnp.float32)
    high = jnp.zeros((1, HEAD), jnp.float32)
    for d in range(4):
        under = jnp.sum((docs < d).astype(jnp.float32), axis=1, keepdims=True)
        upto = jnp.sum((docs <= d).astype(jnp.float32), axis=1, keepdims=True)
        low = jnp.where(lane == d, under, low)
        high = jnp.where(lane == d, upto, high)
    low = jnp.where(low >= GAP, low + (ROWS - TOK), low)
    high = jnp.where(high > GAP, high + (ROWS - TOK), high)
    row_at = lax.broadcasted_iota(jnp.int32, (ROWS, HEAD), 0).astype(jnp.float32)
    token = (row_at < GAP) | (row_at >= GAP + ROWS - TOK)
    inside = (row_at >= low) & (row_at < high) & token
    q_mark = jnp.where(inside, FAR, 0.0).astype(jnp.bfloat16)
    for h in range(HEADS):
        qbuf[h, :, 0:HEAD] = padded(qry[:, h * HEAD:(h + 1) * HEAD])
        qbuf[h, :, HEAD:2 * HEAD] = q_mark
    vx[:, HEAD:2 * HEAD] = jnp.ones((4 * ROWS, HEAD), jnp.bfloat16)
    for cp in loads[3:]:
        cp.wait()

    carry_on(0, 0)
    got(over[0])
    go(over[2])
    spread(1, 0)
    carry_on(0, 1)
    got(over[1])
    go(over[3])
    spread(1, 1)
    carry_on(1, 0)
    got(over[2])
    spread(1, 2)
    carry_on(1, 1)
    got(over[3])
    spread(1, 3)

    whose = [(x * 2 + zh), ((x + 3) % 4) * 2 + zh, ((x + 1) % 4) * 2 + zh, ((x + 2) % 4) * 2 + zh]
    whose = whose + [w + 1 - 2 * zh for w in whose]

    def project(c):
        first, rows = CUT[c]
        part = jnp.zeros((rows, HEAD), jnp.float32)
        for slot in range(8):
            block = rbuf[slot, first:first + rows, :].astype(jnp.float32)
            term = (block - mean[whose[slot]]) * read[whose[slot]]
            for j in range(WIDTH // HEAD):
                part = part + term[:, j * HEAD:(j + 1) * HEAD]
        coef = jnp.sum(part, axis=1, keepdims=True)
        total = jnp.zeros((rows, 2 * HEAD), jnp.float32)
        for slot in range(8):
            block = rbuf[slot, first:first + rows, :].astype(jnp.float32)
            erased = (block - coef * drop[whose[slot]]).astype(jnp.bfloat16)
            weight = wbuf[pl.ds(pl.multiple_of(whose[slot] * WIDTH, WIDTH), WIDTH), :]
            total = total + jnp.dot(erased, weight, preferred_element_type=jnp.float32)
        if first == 0:
            at = lax.broadcasted_iota(jnp.int32, (rows, 2 * HEAD), 0)
            blank = jnp.zeros((1, HEAD), jnp.float32)
            low2 = jnp.concatenate([low, blank], axis=1)
            high2 = jnp.concatenate([high, blank], axis=1)
            total = jnp.where(at >= GAP, jnp.where(at == GAP, low2, jnp.where(at == GAP + 1, high2, 0.0)), total)
        kvbuf[OWN, first:first + rows, :] = total.astype(jnp.bfloat16)

    up = [copy(kvbuf, OWN, 0, cut, above) for cut in CUT]
    up2 = [copy(kvbuf, 0, 1, cut, above) for cut in CUT]
    near = [
        [copy(kvbuf, jnp.where(y + d < YN, OWN, 0), 4 * d, cut, ring(d)) for cut in CUT]
        for d in range(1, YN)
    ]
    far = [[copy(kvbuf, 4 * d, 4 * d + 1, cut, above) for cut in CUT] for d in range(1, YN)]
    side = [copy(kvbuf, OWN, MATE, cut, mate) for cut in CUT]
    used_side = [used[0]]

    def pair(d, c):
        i = used[0]
        used[0] += 1
        first, rows = CUT[c]
        return pltpu.make_async_remote_copy(
            src_ref=kvbuf.at[pl.ds(4 * d, 2), pl.ds(first, rows)],
            dst_ref=kvbuf.at[pl.ds(4 * d + 2, 2), pl.ds(first, rows)],
            send_sem=ssem.at[i],
            recv_sem=rsem.at[i],
            device_id=mate,
            device_id_type=MESH,
        )

    pairs = [[pair(d, c) for c in range(2)] for d in range(YN)]
    order = sorted(range(1, YN), key=lambda d: min(d, YN - d))

    def share(c):
        go(up[c], has_above)
        for d in order:
            go(near[d - 1][c], y + d < YN)
        go(side[c], core == 0)

    def wrapped(c):
        got(up[c], has_below)
        go(up2[c], has_above)
        for d in order:
            go(near[d - 1][c], y + d >= YN)

    def relay(c, d):
        got(near[d - 1][c])
        go(far[d - 1][c], has_above)

    rest(0, 0)
    rest(1, 0)
    rest(1, 1)
    carry_on(1, 2)
    project(0)
    share(0)
    carry_on(1, 3)
    wrapped(0)
    rest(0, 1)
    rest(1, 2)
    rest(1, 3)
    project(1)
    share(1)
    def attend(blocks, start=False):
        keys = sum(rows for _, (_, rows) in blocks)
        at = 0
        for slot, (first, rows) in blocks:
            put = slice(at, at + rows)
            at += rows
            block = kvbuf[slot, first:first + rows, :]
            kx[put, 0:HEAD] = block[:, 0:HEAD]
            vx[put, 0:HEAD] = block[:, HEAD:2 * HEAD]
            mark = kvbuf[slot, GAP - 8:GAP + 8, 0:HEAD].astype(jnp.float32)
            here = slice(first, first + rows)
            seen = (row_at[here] >= mark[8:9]) & (row_at[here] < mark[9:10]) & token[here]
            kx[put, HEAD:2 * HEAD] = jnp.where(seen, 0.0, 1.0).astype(jnp.bfloat16)

        score = lax.dot_general(
            qbuf[...].reshape(HEADS * ROWS, 2 * HEAD), kx[0:keys], (((1,), (1,)), ((), ())),
            preferred_element_type=jnp.float32,
        )
        if start:
            shape = (HEADS, ROWS, keys)
            q_at = lax.broadcasted_iota(jnp.int32, shape, 1).reshape(HEADS * ROWS, keys)
            k_at = lax.broadcasted_iota(jnp.int32, shape, 2).reshape(HEADS * ROWS, keys)
            score = jnp.where((k_at <= q_at) | (k_at >= ROWS), score, FAR)
        tiles = [score[:, i:i + HEAD] for i in range(0, keys, HEAD)]
        rough = functools.reduce(jnp.maximum, tiles[1:], tiles[0]) if keys % HEAD == 0 else score
        best = jnp.max(rough, axis=1, keepdims=True)
        if start:
            best = jnp.broadcast_to(best, (HEADS * ROWS, HEAD))
            expo = jnp.exp2((score - best[:, 0:1]) * (SCALE * LOG2E)).astype(jnp.bfloat16)
        else:
            old = top[...]
            best = jnp.maximum(best, old)
            wide = jnp.concatenate([best] * len(tiles), axis=1)
            expo = jnp.exp2((score - wide) * (SCALE * LOG2E)).astype(jnp.bfloat16)
        mixed = jnp.dot(expo, vx[0:keys], preferred_element_type=jnp.float32)
        if not start:
            factor = jnp.exp2((old - best) * (SCALE * LOG2E))
            mixed = mixed + acc[...] * jnp.concatenate([factor, factor], axis=1)
        acc[...] = mixed
        top[...] = best

    calls = ((0, 1), (YN - 1, 2), (YN - 2, 3), (YN - 3, 4))

    def to_mate(c, n):
        for d in calls[n]:
            if d == 0:
                got(up2[c], has_below)
            else:
                got(far[d - 1][c], has_below)
            go(pairs[d][c])

    def take(c, n):
        for d in calls[n]:
            got(pairs[d][c])
        attend([(4 * d + j, CUT[c]) for d in calls[n] for j in range(4)])

    for d in order:
        relay(0, d)
    wrapped(1)
    to_mate(0, 0)
    for c in range(2):
        got(side[c], core == 1)
    attend([(OWN, (0, ROWS)), (MATE, (0, ROWS))], True)
    to_mate(0, 1)
    take(0, 0)
    to_mate(0, 2)
    relay(1, order[0])
    relay(1, order[1])
    take(0, 1)
    to_mate(0, 3)
    relay(1, order[2])
    relay(1, order[3])
    take(0, 2)
    for d in order[4:]:
        relay(1, d)
    to_mate(1, 0)
    take(0, 3)
    for n in range(4):
        if n < 3:
            to_mate(1, n + 1)
        take(1, n)

    for h in range(HEADS):
        both = acc[h * ROWS:(h + 1) * ROWS]
        mean_value = (both[:, 0:HEAD] / both[:, HEAD:2 * HEAD])
        kept = jnp.concatenate([mean_value[:GAP], mean_value[GAP + ROWS - TOK:]], axis=0)
        out[:, h * HEAD:(h + 1) * HEAD] = kept.astype(jnp.bfloat16)

    for cp, when in sent:
        if when is None:
            cp.wait_send()
        else:
            pl.when(when)(cp.wait_send)


def on_device(residual, mean_vec, proj_u, proj_v, key_weight, value_weight, queries, doc_ids):
    whole = pl.BlockSpec(memory_space=pltpu.VMEM)
    hbm = pl.BlockSpec(memory_space=pltpu.HBM)
    flat = (8, 1, WIDTH)
    return pl.pallas_call(
        kernel,
        out_shape=jax.ShapeDtypeStruct((TOK, WIDTH), jnp.bfloat16),
        in_specs=[hbm] * 8,
        out_specs=whole,
        scratch_shapes=[
            pltpu.VMEM((TOK, WIDTH), jnp.bfloat16),
            pltpu.VMEM(flat, jnp.float32),
            pltpu.VMEM(flat, jnp.float32),
            pltpu.VMEM(flat, jnp.float32),
            pltpu.VMEM((TOK, WIDTH), jnp.bfloat16),
            pltpu.VMEM((1, TOK), jnp.int32),
            pltpu.VMEM((8, ROWS, WIDTH), jnp.bfloat16),
            pltpu.VMEM((8 * WIDTH, 2 * HEAD), jnp.bfloat16),
            pltpu.VMEM((SLOTS, ROWS, 2 * HEAD), jnp.bfloat16),
            pltpu.VMEM((HEADS, ROWS, 2 * HEAD), jnp.bfloat16),
            pltpu.VMEM((4 * ROWS, 2 * HEAD), jnp.bfloat16),
            pltpu.VMEM((4 * ROWS, 2 * HEAD), jnp.bfloat16),
            pltpu.VMEM((HEADS * ROWS, 2 * HEAD), jnp.float32),
            pltpu.VMEM((HEADS * ROWS, HEAD), jnp.float32),
            pltpu.SemaphoreType.DMA((SEMS,)),
            pltpu.SemaphoreType.DMA((SEMS,)),
            pltpu.SemaphoreType.DMA((8,)),
        ],
        compiler_params=pltpu.CompilerParams(
            collective_id=0, has_side_effects=True, vmem_limit_bytes=60 << 20
        ),
    )(
        residual, mean_vec.reshape(flat), proj_u.reshape(flat), proj_v.reshape(flat),
        key_weight, value_weight, queries, doc_ids.reshape(1, TOK),
    )


def solution(mesh):
    return jax.shard_map(
        on_device,
        mesh=mesh,
        in_specs=(
            P("seq", "tensor"), P(), P(), P(), P(None, "tensor"), P(None, "tensor"),
            P("seq", "tensor"), P("seq"),
        ),
        out_specs=P("seq", "tensor"),
        check_vma=False,
    )
```

time: 118 us -> 72.7 us (0.62)
  Pallas kernels: 108 us -> 70.8 us
  local copies, waits for them, and re-layouts: 8.79 us -> 1.71 us
    pallas_call x1, Pallas kernels: 108 us -> 70.8 us  [on_device(): pl.pallas_call(kernel, out_shape=jax.ShapeDtypeStruct((TOK, WIDTH), jnp.b...]
    unnamed x17 -> x1, local copies, waits for them, and re-layouts: 8.79 us -> 1.71 us
where the time goes in v2:
time: 72.7 us; the launch traced here: 72.6 us
  Pallas kernels  70.8 us (97%)
  local copies, waits for them, and re-layouts  1.71 us (2%)
    pallas_call x1, Pallas kernels, on_device(): pl.pallas_call(kernel, out_shape=jax.ShapeDtypeStruct((TOK, WIDTH), jnp.b...  70.8 us
    unnamed x1, local copies, waits for them, and re-layouts  1.71 us

profile of v2, /device:TPU:192, one launch (start us, length us, event | category | flops | bytes accessed | tf_op | source)
XLA Modules:
  0.0 72.6 jit_solution(3110074621639102034)
XLA Ops:
  0.0 70.8 %shard_map.82 = bf16[152,1024]{1,0:T(8,128)(2,1)} custom-call(bf16[152,1024]{1,0:T(8,128)(2,1)} %res_hbm.1, f32[8,1,1024]{2,1,0:T(1,128)} %bitcast.4, f32[8,1,1024]{2,1,0:T(1,128)} %bitcast.5, f32[8,1,1024]{2,1,0:T(1,128)} %bitcast.6, bf16[8192,128]{1,0:T(8,128)(2,1)} %wk_hbm.1, bf16[8192,128]{1,0:T(8,128)(2,1)} %wv_hbm.1, bf16[152,1024]{1,0:T(8,128)(2,1)} %qry_hbm.1, ...), custom_call_target="tpu_custom_call" | custom-call | tf_op jit(solution)/shard_map/pallas_call | solution.py:376
  70.8 1.7 %copy.10 = bf16[152,1024]{1,0:T(8,128)(2,1)} copy(bf16[152,1024]{1,0:T(8,128)(2,1)} %shard_map.82) | data formatting | bytes 622592

commit v3 on v2

--- a/solution.py
+++ b/solution.py
@@ -10,9 +10,8 @@
 HEAD = 128
 TOK = 152
 ROWS = 160
-GAP = 72
-CUT = ((0, 80), (80, 80))
-PIECE = ((0, 48), (48, 32), (80, 48), (128, 32))
+GAP = 40
+CUT = ((0, 48), (48, 64), (112, 48))
 WIDTH = 1024
 YN = 8
 SCALE = 1.0 / HEAD**0.5
@@ -21,7 +20,8 @@
 MESH = pl.DeviceIdType.MESH
 OWN, MATE = 4 * YN, 4 * YN + 1
 SLOTS = 4 * YN + 2
-SEMS = 96
+SEMS = 112
+KEYS = 1024
 
 
 def kernel(
@@ -39,6 +39,7 @@
 
     right = dev((x + 1) % 4, zh, zl, y, core)
     left = dev((x + 3) % 4, zh, zl, y, core)
+    facing = dev((x + 2) % 4, zh, zl, y, core)
     across = dev(x, 1 - zh, zl, y, core)
     above = dev(x, zh, (zl + 1) % 4, y, core)
     below = dev(x, zh, (zl + 3) % 4, y, core)
@@ -53,7 +54,7 @@
     def hello(device):
         pl.semaphore_signal(bar, inc=1, device_id=device, device_id_type=MESH)
 
-    for device in [right, left, across, mate] + [ring(d) for d in range(1, YN)]:
+    for device in [right, left, facing, across, mate] + [ring(d) for d in range(1, YN)]:
         hello(device)
 
     @pl.when(has_above)
@@ -94,7 +95,7 @@
     loads[0].wait()
     rbuf[0] = padded(res[...])
 
-    peers = 4 + YN - 1 + jnp.where(has_above, 1, 0) + jnp.where(has_below, 1, 0)
+    peers = 5 + YN - 1 + jnp.where(has_above, 1, 0) + jnp.where(has_below, 1, 0)
     pl.semaphore_wait(bar, peers)
 
     used = [0]
@@ -126,34 +127,46 @@
         else:
             pl.when(when)(cp.wait_recv)
 
-    over = [copy(rbuf, 0, 4, cut, across) for cut in PIECE]
-    to_right = [[copy(rbuf, 4 * h, 4 * h + 1, cut, right) for cut in (CUT, PIECE)[h]] for h in range(2)]
-    to_left = [[copy(rbuf, 4 * h, 4 * h + 2, cut, left) for cut in (CUT, PIECE)[h]] for h in range(2)]
-    rightward = ((True, False), (True, False, False, True))
+    over = [copy(rbuf, 0, 4, cut, across) for cut in CUT]
+    to_right = [[copy(rbuf, 4 * h, 4 * h + 1, cut, right) for cut in CUT] for h in range(2)]
+    to_left = [[copy(rbuf, 4 * h, 4 * h + 2, cut, left) for cut in CUT] for h in range(2)]
+    rightward = ((True, False, False), (False, True, True))
     onward = [
         [
             copy(rbuf, 4 * h + 1, 4 * h + 3, cut, right) if way else copy(rbuf, 4 * h + 2, 4 * h + 3, cut, left)
-            for way, cut in zip(rightward[h], (CUT, PIECE)[h])
+            for way, cut in zip(rightward[h], CUT)
         ]
         for h in range(2)
     ]
 
+    hop2 = [[copy(rbuf, 4 * h, 4 * h + 3, cut, facing) for cut in CUT] for h in range(2)]
+    is_direct = ((False, False, False), (True, True, True))
+
     def spread(h, p):
         go(to_right[h][p])
         go(to_left[h][p])
+        if is_direct[h][p]:
+            go(hop2[h][p])
 
     def carry_on(h, p):
+        if is_direct[h][p]:
+            return
         got((to_right if rightward[h][p] else to_left)[h][p])
         go(onward[h][p])
 
     def rest(h, p):
+        if is_direct[h][p]:
+            got(to_left[h][p])
+            got(to_right[h][p])
+            got(hop2[h][p])
+            return
         got((to_left if rightward[h][p] else to_right)[h][p])
         got(onward[h][p])
 
-    go(over[0])
+    over[0].start()
     spread(0, 0)
-    go(over[1])
     spread(0, 1)
+    spread(0, 2)
     for cp in loads[1:3]:
         cp.wait()
     lane = lax.broadcasted_iota(jnp.int32, (1, HEAD), 1)
@@ -174,24 +187,19 @@
     for h in range(HEADS):
         qbuf[h, :, 0:HEAD] = padded(qry[:, h * HEAD:(h + 1) * HEAD])
         qbuf[h, :, HEAD:2 * HEAD] = q_mark
-    vx[:, HEAD:2 * HEAD] = jnp.ones((4 * ROWS, HEAD), jnp.bfloat16)
+    vx[:, HEAD:2 * HEAD] = jnp.ones((KEYS, HEAD), jnp.bfloat16)
     for cp in loads[3:]:
         cp.wait()
 
+    over[0].wait_send()
+    over[1].start()
     carry_on(0, 0)
+    carry_on(0, 1)
+    over[1].wait_send()
+    go(over[2])
+    carry_on(0, 2)
     got(over[0])
-    go(over[2])
     spread(1, 0)
-    carry_on(0, 1)
-    got(over[1])
-    go(over[3])
-    spread(1, 1)
-    carry_on(1, 0)
-    got(over[2])
-    spread(1, 2)
-    carry_on(1, 1)
-    got(over[3])
-    spread(1, 3)
 
     whose = [(x * 2 + zh), ((x + 3) % 4) * 2 + zh, ((x + 1) % 4) * 2 + zh, ((x + 2) % 4) * 2 + zh]
     whose = whose + [w + 1 - 2 * zh for w in whose]
@@ -227,7 +235,6 @@
     ]
     far = [[copy(kvbuf, 4 * d, 4 * d + 1, cut, above) for cut in CUT] for d in range(1, YN)]
     side = [copy(kvbuf, OWN, MATE, cut, mate) for cut in CUT]
-    used_side = [used[0]]
 
     def pair(d, c):
         i = used[0]
@@ -242,7 +249,7 @@
             device_id_type=MESH,
         )
 
-    pairs = [[pair(d, c) for c in range(2)] for d in range(YN)]
+    pairs = [[pair(d, c) for c in range(len(CUT))] for d in range(YN)]
     order = sorted(range(1, YN), key=lambda d: min(d, YN - d))
 
     def share(c):
@@ -261,20 +268,7 @@
         got(near[d - 1][c])
         go(far[d - 1][c], has_above)
 
-    rest(0, 0)
-    rest(1, 0)
-    rest(1, 1)
-    carry_on(1, 2)
-    project(0)
-    share(0)
-    carry_on(1, 3)
-    wrapped(0)
-    rest(0, 1)
-    rest(1, 2)
-    rest(1, 3)
-    project(1)
-    share(1)
-    def attend(blocks, start=False):
+    def attend(blocks, start=False, own=False):
         keys = sum(rows for _, (_, rows) in blocks)
         at = 0
         for slot, (first, rows) in blocks:
@@ -292,22 +286,23 @@
             qbuf[...].reshape(HEADS * ROWS, 2 * HEAD), kx[0:keys], (((1,), (1,)), ((), ())),
             preferred_element_type=jnp.float32,
         )
-        if start:
+        if own:
             shape = (HEADS, ROWS, keys)
             q_at = lax.broadcasted_iota(jnp.int32, shape, 1).reshape(HEADS * ROWS, keys)
             k_at = lax.broadcasted_iota(jnp.int32, shape, 2).reshape(HEADS * ROWS, keys)
             score = jnp.where((k_at <= q_at) | (k_at >= ROWS), score, FAR)
-        tiles = [score[:, i:i + HEAD] for i in range(0, keys, HEAD)]
-        rough = functools.reduce(jnp.maximum, tiles[1:], tiles[0]) if keys % HEAD == 0 else score
+        cuts = [score[:, i:i + HEAD] for i in range(0, keys, HEAD)]
+        whole = [tile for tile in cuts if tile.shape[1] == HEAD]
+        rough = functools.reduce(jnp.maximum, whole)
         best = jnp.max(rough, axis=1, keepdims=True)
-        if start:
-            best = jnp.broadcast_to(best, (HEADS * ROWS, HEAD))
-            expo = jnp.exp2((score - best[:, 0:1]) * (SCALE * LOG2E)).astype(jnp.bfloat16)
-        else:
+        if len(whole) < len(cuts):
+            best = jnp.maximum(best, jnp.max(cuts[-1], axis=1, keepdims=True))
+        best = jnp.broadcast_to(best, (HEADS * ROWS, HEAD))
+        if not start:
             old = top[...]
             best = jnp.maximum(best, old)
-            wide = jnp.concatenate([best] * len(tiles), axis=1)
-            expo = jnp.exp2((score - wide) * (SCALE * LOG2E)).astype(jnp.bfloat16)
+        wide = jnp.concatenate([best[:, :tile.shape[1]] for tile in cuts], axis=1)
+        expo = jnp.exp2((score - wide) * (SCALE * LOG2E)).astype(jnp.bfloat16)
         mixed = jnp.dot(expo, vx[0:keys], preferred_element_type=jnp.float32)
         if not start:
             factor = jnp.exp2((old - best) * (SCALE * LOG2E))
@@ -315,46 +310,69 @@
         acc[...] = mixed
         top[...] = best
 
-    calls = ((0, 1), (YN - 1, 2), (YN - 2, 3), (YN - 3, 4))
-
-    def to_mate(c, n):
-        for d in calls[n]:
+    pool = [0] + order
+
+    def to_mate(c, *groups):
+        for d in groups:
             if d == 0:
                 got(up2[c], has_below)
             else:
                 got(far[d - 1][c], has_below)
             go(pairs[d][c])
 
-    def take(c, n):
-        for d in calls[n]:
+    def take(c, *groups, start=False):
+        for d in groups:
             got(pairs[d][c])
-        attend([(4 * d + j, CUT[c]) for d in calls[n] for j in range(4)])
-
-    for d in order:
-        relay(0, d)
+        attend([(4 * d + j, CUT[c]) for d in groups for j in range(4)], start)
+
+    def relays(c, *groups):
+        for d in groups:
+            relay(c, d)
+
+    carry_on(1, 0)
+    got(over[1])
+    spread(1, 1)
+    rest(0, 0)
+    rest(1, 0)
+    project(0)
+    share(0)
+    carry_on(1, 1)
+    got(over[2])
+    spread(1, 2)
+    wrapped(0)
+    rest(0, 1)
+    rest(1, 1)
+    project(1)
+    share(1)
+    carry_on(1, 2)
+    relays(0, *order)
+    to_mate(0, *pool[:4])
     wrapped(1)
-    to_mate(0, 0)
-    for c in range(2):
+    rest(0, 2)
+    rest(1, 2)
+    project(2)
+    share(2)
+    to_mate(0, *pool[4:])
+    take(0, *pool[0:2], start=True)
+    relays(1, *order[:3])
+    take(0, *pool[2:4])
+    wrapped(2)
+    relays(1, *order[3:])
+    take(0, *pool[4:6])
+    to_mate(1, *pool[:4])
+    take(0, *pool[6:8])
+    relays(2, *order[:3])
+    to_mate(1, *pool[4:])
+    for c in range(3):
         got(side[c], core == 1)
-    attend([(OWN, (0, ROWS)), (MATE, (0, ROWS))], True)
-    to_mate(0, 1)
-    take(0, 0)
-    to_mate(0, 2)
-    relay(1, order[0])
-    relay(1, order[1])
-    take(0, 1)
-    to_mate(0, 3)
-    relay(1, order[2])
-    relay(1, order[3])
-    take(0, 2)
-    for d in order[4:]:
-        relay(1, d)
-    to_mate(1, 0)
-    take(0, 3)
-    for n in range(4):
-        if n < 3:
-            to_mate(1, n + 1)
-        take(1, n)
+    attend([(OWN, (0, ROWS)), (MATE, (0, ROWS))], own=True)
+    relays(2, *order[3:])
+    take(1, *pool[:4])
+    to_mate(2, *pool[:4])
+    take(1, *pool[4:])
+    to_mate(2, *pool[4:])
+    take(2, *pool[:4])
+    take(2, *pool[4:])
 
     for h in range(HEADS):
         both = acc[h * ROWS:(h + 1) * ROWS]
@@ -389,8 +407,8 @@
             pltpu.VMEM((8 * WIDTH, 2 * HEAD), jnp.bfloat16),
             pltpu.VMEM((SLOTS, ROWS, 2 * HEAD), jnp.bfloat16),
             pltpu.VMEM((HEADS, ROWS, 2 * HEAD), jnp.bfloat16),
-            pltpu.VMEM((4 * ROWS, 2 * HEAD), jnp.bfloat16),
-            pltpu.VMEM((4 * ROWS, 2 * HEAD), jnp.bfloat16),
+            pltpu.VMEM((KEYS, 2 * HEAD), jnp.bfloat16),
+            pltpu.VMEM((KEYS, 2 * HEAD), jnp.bfloat16),
             pltpu.VMEM((HEADS * ROWS, 2 * HEAD), jnp.float32),
             pltpu.VMEM((HEADS * ROWS, HEAD), jnp.float32),
             pltpu.SemaphoreType.DMA((SEMS,)),

time: 72.7 us -> 69.3 us (0.953)
  the two profiles are of different devices: /device:TPU:192 before, /device:TPU:202 now
where the time goes in v3:
time: 69.3 us; the launch traced here: 69.1 us
  Pallas kernels  67.4 us (97%)
  local copies, waits for them, and re-layouts  1.71 us (2%)
    pallas_call x1, Pallas kernels, on_device(): pl.pallas_call(kernel, out_shape=jax.ShapeDtypeStruct((TOK, WIDTH), jnp.b...  67.4 us
    unnamed x1, local copies, waits for them, and re-layouts  1.71 us

profile of v3, /device:TPU:202, one launch (start us, length us, event | category | flops | bytes accessed | tf_op | source)
XLA Modules:
  0.0 69.1 jit_solution(1918332116058695367)
XLA Ops:
  0.0 67.4 %shard_map.82 = bf16[152,1024]{1,0:T(8,128)(2,1)} custom-call(bf16[152,1024]{1,0:T(8,128)(2,1)} %res_hbm.1, f32[8,1,1024]{2,1,0:T(1,128)} %bitcast.4, f32[8,1,1024]{2,1,0:T(1,128)} %bitcast.5, f32[8,1,1024]{2,1,0:T(1,128)} %bitcast.6, bf16[8192,128]{1,0:T(8,128)(2,1)} %wk_hbm.1, bf16[8192,128]{1,0:T(8,128)(2,1)} %wv_hbm.1, bf16[152,1024]{1,0:T(8,128)(2,1)} %qry_hbm.1, ...), custom_call_target="tpu_custom_call" | custom-call | tf_op jit(solution)/shard_map/pallas_call | solution.py:394
  67.4 1.7 %copy.10 = bf16[152,1024]{1,0:T(8,128)(2,1)} copy(bf16[152,1024]{1,0:T(8,128)(2,1)} %shard_map.82) | data formatting | bytes 622592

commit v4 on v3

--- a/solution.py
+++ b/solution.py
@@ -353,14 +353,11 @@
     project(2)
     share(2)
     to_mate(0, *pool[4:])
-    take(0, *pool[0:2], start=True)
-    relays(1, *order[:3])
-    take(0, *pool[2:4])
+    take(0, *pool[0:4], start=True)
+    relays(1, *order)
     wrapped(2)
-    relays(1, *order[3:])
-    take(0, *pool[4:6])
+    take(0, *pool[4:8])
     to_mate(1, *pool[:4])
-    take(0, *pool[6:8])
     relays(2, *order[:3])
     to_mate(1, *pool[4:])
     for c in range(3):

time: 69.3 us -> 70.6 us (1.019)
  the two profiles are of different devices: /device:TPU:202 before, /device:TPU:66 now
where the time goes in v4:
time: 70.6 us; the launch traced here: 70.5 us
  Pallas kernels  68.7 us (97%)
  local copies, waits for them, and re-layouts  1.71 us (2%)
    pallas_call x1, Pallas kernels, on_device(): pl.pallas_call(kernel, out_shape=jax.ShapeDtypeStruct((TOK, WIDTH), jnp.b...  68.7 us
    unnamed x1, local copies, waits for them, and re-layouts  1.71 us

profile of v4, /device:TPU:66, one launch (start us, length us, event | category | flops | bytes accessed | tf_op | source)
XLA Modules:
  0.0 70.5 jit_solution(13696981313390114254)
XLA Ops:
  0.0 68.7 %shard_map.82 = bf16[152,1024]{1,0:T(8,128)(2,1)} custom-call(bf16[152,1024]{1,0:T(8,128)(2,1)} %res_hbm.1, f32[8,1,1024]{2,1,0:T(1,128)} %bitcast.4, f32[8,1,1024]{2,1,0:T(1,128)} %bitcast.5, f32[8,1,1024]{2,1,0:T(1,128)} %bitcast.6, bf16[8192,128]{1,0:T(8,128)(2,1)} %wk_hbm.1, bf16[8192,128]{1,0:T(8,128)(2,1)} %wv_hbm.1, bf16[152,1024]{1,0:T(8,128)(2,1)} %qry_hbm.1, ...), custom_call_target="tpu_custom_call" | custom-call | tf_op jit(solution)/shard_map/pallas_call | solution.py:391
  68.7 1.7 %copy.10 = bf16[152,1024]{1,0:T(8,128)(2,1)} copy(bf16[152,1024]{1,0:T(8,128)(2,1)} %shard_map.82) | data formatting | bytes 622592
